TPU v7x, 512 devices: a whole 4x4x16 slice. The times are simulated.
512 devices in a mesh: row: 16 (over y, z_hi, core), col: 32 (over x, z_lo).
Axes of the slice: x: 4, y: 4, z: 16 (z_hi: 2, z_lo: 8; z = z_hi * 8 + z_lo), core: 2. Of those that a mesh axis runs over, the one named last changes fastest.
Arguments:
- observed: bfloat16 [32768, 128], P(('row', 'col')), may hold values from -6 to 6
- prior_mean: bfloat16 [32768, 128], P(('row', 'col')), may hold values from -6 to 6
- missing: int32 [32768, 128], P(('row', 'col')), may hold values 0 or 1
- eigvec: bfloat16 [32768, 32768], P('row', 'col'), may hold values from -0.0625 to 0.0625
- lam_space: float32 [32768], P('col'), may hold values from 0.1 to 10
- lam_time: float32 [32], replicated, may hold values from 0.1 to 10
Outputs:
- smoothed: float32 [32768, 128], P(('row', 'col'))
All inputs are finite; a program needn't handle non-finite values. No bound on the sum of `missing` on one device may be relied on, other than what follows from the above.
Results may differ from a plain program's by a relative error of at most 0.0022.
Values may be sent and summed in bfloat16 or wider, within the bound.
No kernel may reach another device: no remote copies, remote signals or barrier semaphores. Data moves between devices by JAX's collectives and lax.ppermute only.
A program may use at most 64 MiB of HBM per device.

v0:
```python
import math

import jax
import jax.numpy as jnp
from jax import lax
from jax.sharding import PartitionSpec as P

MONTHS = 32
VARS = 4


def cosine_table():
    freq = jnp.arange(MONTHS, dtype=jnp.float32)[:, None]
    month = jnp.arange(MONTHS, dtype=jnp.float32)[None, :]
    table = jnp.cos(math.pi * (month + 0.5) * freq / MONTHS) * math.sqrt(2.0 / MONTHS)
    first = jnp.where(jnp.arange(MONTHS)[:, None] == 0, 1.0 / math.sqrt(2.0), 1.0)
    return table * first


def shrink(proj, lam_space, lam_time):
    count = proj.shape[0]
    table = cosine_table()
    blocks = proj.reshape(count, VARS, MONTHS)
    spec = jnp.einsum("kvm,jm->kvj", blocks, table, precision=lax.Precision.HIGHEST)
    gain = lam_space[:, None] * lam_time[None, :]
    gain = gain / (gain + 1.0)
    scaled = spec * gain[:, None, :]
    back = jnp.einsum("kvj,jm->kvm", scaled, table, precision=lax.Precision.HIGHEST)
    return back.reshape(count, VARS * MONTHS).astype(jnp.bfloat16)


def shards(observed, prior_mean, missing, eigvec, lam_space, lam_time):
    filled = jnp.where(missing == 1, prior_mean, observed)
    station_part = eigvec
    proj = lax.dot_general(
        station_part,
        lax.all_gather(filled, "col", axis=0, tiled=True),
        (((0,), (0,)), ((), ())),
        preferred_element_type=jnp.float32,
    )
    total_proj = lax.psum(proj, "row")
    coeffs = shrink(total_proj, lam_space, lam_time)
    station_part = eigvec
    return lax.psum_scatter(
        jnp.dot(station_part, coeffs, preferred_element_type=jnp.float32),
        "col",
        scatter_dimension=0,
        tiled=True,
    )


def solution(mesh):
    in_specs = (
        P(("row", "col"), None),
        P(("row", "col"), None),
        P(("row", "col"), None),
        P("row", "col"),
        P("col"),
        P(),
    )
    out_specs = P(("row", "col"), None)
    return jax.shard_map(shards, mesh=mesh, in_specs=in_specs, out_specs=out_specs, check_vma=False)
```

profile of v0, /device:TPU:8, one launch (start us, length us, event | category | flops | bytes accessed | tf_op | source)
XLA Modules:
  0.0 648.7 jit_solution(13733486362954848152)
XLA Ops:
  6.5 0.0 copy-start.1
  6.5 0.0 copy-start
  6.5 0.0 all-reduce.2.cloned.1.call-start
  6.5 0.8 compare_select_fusion
  7.4 129.3 %all_gather.3 = bf16[2048,128]{1,0:T(8,128)(2,1)S(1)} all-gather(bf16[64,128]{1,0:T(8,128)(2,1)S(1)} %compare_select_fusion), channel_id=1, replica_groups=mesh['row'=16,'col'=32] {'col'}, dimensions={0}, use_global_device_ids=true | all-gather | bytes 540672 | tf_op jit(solution)/shard_map/all_gather | solution.py:37
  136.6 3.7 fusion.11
  140.4 0.0 all-reduce.2.cloned.1.call-update
  140.4 0.0 reduce-scatter.4.cloned.1.call-start
  140.5 0.0 copy-done.1
  140.5 0.0 copy-done
  140.5 0.1 add_divide_fusion
  140.6 241.9 %all-reduce.2.cloned.1.call-done = f32[1024,4,32]{0,2,1:T(8,128)} async-done(((f32[1024,4,32]{0,2,1:T(8,128)}), f32[1024,4,32]{0,2,1:T(8,128)}) %all-reduce.2.cloned.1.call-update) | async-done | bytes 524304 | tf_op jit(solution)/shard_map/psum | solution.py:41
  382.5 1.8 convolution_multiply_fusion
  384.3 0.7 convolution_convert_fusion
  385.0 3.7 convolution_bitcast_fusion
  388.7 1.3 copy.9
  390.0 0.0 reduce-scatter.4.cloned.1.call-update
  390.0 251.8 %reduce-scatter.4.cloned.1.call-done = f32[64,128]{1,0:T(8,128)} async-done(((f32[2048,128]{1,0:T(8,128)}), f32[64,128]{1,0:T(8,128)}) %reduce-scatter.4.cloned.1.call-update) | async-done | bytes 32784 | tf_op jit(solution)/shard_map/reduce_scatter | solution.py:44
  (1 shorter events, 0.0 us)
Async XLA Ops:
  6.5 133.9 %copy-start.1 = (f32[32]{0:T(128)S(1)}, f32[32]{0:T(128)}, u32[]{:S(2)}) copy-start(f32[32]{0:T(128)} %param.11) | copy-start | bytes 388
  6.5 133.9 %copy-start = (f32[1024]{0:T(1024)S(1)}, f32[1024]{0:T(1024)}, u32[]{:S(2)}) copy-start(f32[1024]{0:T(1024)} %param.10) | copy-start | bytes 12292
  6.5 375.9 %all-reduce.2.cloned.1.call-start = ((), (), s32[]{:S(2)}) async-start(), calls=%async_computation.1 | async-start | bytes 1048576 | tf_op jit(solution)/shard_map/psum | solution.py:41
  140.4 501.5 %reduce-scatter.4.cloned.1.call-start = ((), (), s32[]{:S(2)}) async-start(), calls=%async_computation.2 | async-start | bytes 1081344 | tf_op jit(solution)/shard_map/reduce_scatter | solution.py:44
Sparse Core Ops, SparseCore 0:
  140.5 241.8 all-reduce.1
  390.2 251.6 reduce-scatter.3
where the time goes:
time: 649 us
  waiting for transfers between devices  494 us (76%)
  blocking collectives  129 us (20%)
  between operations  13.5 us (2%)
  matrix products  9.95 us (2%)
    reduce_scatter x1, waiting for transfers between devices, shards(): lax.psum_scatter(jnp.dot(station_part, coeffs, preferred_element_type=jnp...  252 us
    psum x1, waiting for transfers between devices, shards(): total_proj = lax.psum(proj, 'row')  242 us
    all_gather x1, blocking collectives, shards(): lax.all_gather(filled, 'col', axis=0, tiled=True)  129 us
  transfers between devices with their start and end apart: 2, of which 2 were waited for; matrix products, arithmetic and copies ran while one was open for 0% of the time, Pallas kernels for 0%

commit v1 on v0

v1 whole, which is shorter than its diff:
```python
import math

import jax
import jax.numpy as jnp
from jax import lax
from jax.sharding import Mesh
from jax.sharding import PartitionSpec as P

MONTHS = 32
VARS = 4
ROW = ("y", "zh", "core")
COL = ("x", "zl")
PAIR = ("y", "core")


def cosine_table():
    freq = jnp.arange(MONTHS, dtype=jnp.float32)[:, None]
    month = jnp.arange(MONTHS, dtype=jnp.float32)[None, :]
    table = jnp.cos(math.pi * (month + 0.5) * freq / MONTHS) * math.sqrt(2.0 / MONTHS)
    first = jnp.where(jnp.arange(MONTHS)[:, None] == 0, 1.0 / math.sqrt(2.0), 1.0)
    return table * first


def shrink(proj, lam_space, lam_time):
    count = proj.shape[0]
    table = cosine_table()
    blocks = proj.reshape(count, VARS, MONTHS)
    spec = jnp.einsum("kvm,jm->kvj", blocks, table, precision=lax.Precision.HIGHEST)
    gain = lam_space[:, None] * lam_time[None, :]
    gain = gain / (gain + 1.0)
    scaled = spec * gain[:, None, :]
    back = jnp.einsum("kvj,jm->kvm", scaled, table, precision=lax.Precision.HIGHEST)
    return back.reshape(count, VARS * MONTHS).astype(jnp.bfloat16)


def gather(block, axes):
    size = lax.axis_size(axes)
    copies = jnp.broadcast_to(block, (size,) + block.shape)
    return lax.all_to_all(copies, axes, 0, 0).reshape((size * block.shape[0],) + block.shape[1:])


def scatter_sum(parts, axes):
    size = lax.axis_size(axes)
    pieces = parts.reshape((size, parts.shape[0] // size) + parts.shape[1:])
    return lax.all_to_all(pieces, axes, 0, 0).astype(jnp.float32).sum(0)


def shards(observed, prior_mean, missing, eigvec, lam_space, lam_time):
    filled = jnp.where(missing == 1, prior_mean, observed)
    filled = gather(gather(filled, "zl"), "x")
    proj = lax.dot_general(eigvec, filled, (((0,), (0,)), ((), ())), preferred_element_type=jnp.float32)
    total = scatter_sum(proj, PAIR)
    total = total + lax.ppermute(total, "zh", [(0, 1), (1, 0)])
    count = total.shape[0]
    mine = lax.dynamic_slice_in_dim(lam_space, lax.axis_index(PAIR) * count, count)
    coeffs = gather(shrink(total, mine, lam_time), PAIR)
    part = jnp.dot(eigvec, coeffs, preferred_element_type=jnp.float32).astype(jnp.bfloat16)
    return scatter_sum(scatter_sum(part, "x"), "zl")


def solution(mesh):
    fine = Mesh(mesh.devices.reshape(4, 2, 2, 4, 8), ("y", "zh", "core", "x", "zl"))
    rows = P(ROW + COL, None)
    in_specs = (rows, rows, rows, P(ROW, COL), P(COL), P())
    return jax.shard_map(shards, mesh=fine, in_specs=in_specs, out_specs=rows, check_vma=False)
```

time: 649 us -> 120 us (0.18)
  the two profiles are of different devices: /device:TPU:8 before, /device:TPU:32 now
where the time goes in v1:
time: 120 us; the launch traced here: 119 us
  blocking collectives  76.3 us (64%)
  waiting for transfers between devices  19.3 us (16%)
  starting transfers between devices  12.7 us (11%)
  matrix products  7.37 us (6%)
  local copies, waits for them, and re-layouts  1.99 us (2%)
  other arithmetic  1.62 us (1%)
    all_to_all x3, blocking collectives, gather(): lax.all_to_all(copies, axes, 0, 0)  45.7 us
    all_to_all x2, blocking collectives, scatter_sum(): return lax.all_to_all(pieces, axes, 0, 0).astype(jnp.float32).sum(0)  30.6 us
    ppermute x1, waiting for transfers between devices, shards(): total = total + lax.ppermute(total, 'zh', [(0, 1), (1, 0)])  9.75 us
    all_to_all x1, waiting for transfers between devices, scatter_sum(): return lax.all_to_all(pieces, axes, 0, 0).astype(jnp.float32).sum(0)  9.51 us
    ppermute x1, starting transfers between devices, shards(): total = total + lax.ppermute(total, 'zh', [(0, 1), (1, 0)])  8.23 us
    all_to_all x1, starting transfers between devices, scatter_sum(): return lax.all_to_all(pieces, axes, 0, 0).astype(jnp.float32).sum(0)  4.47 us
    dot_general x1, matrix products, shards(): jnp.dot(eigvec, coeffs, preferred_element_type=jnp.float32)  3.72 us
    dot_general x1, matrix products, shards(): lax.dot_general(eigvec, filled, (((0,), (0,)), ((), ())), preferred_eleme...  2.93 us
  transfers between devices with their start and end apart: 2, of which 2 were waited for; matrix products, arithmetic and copies ran while one was open for 1% of the time, Pallas kernels for 0%

profile of v1, /device:TPU:32, one launch (start us, length us, event | category | flops | bytes accessed | tf_op | source)
XLA Modules:
  0.0 119.3 jit_solution(6120623621936768627)
XLA Ops:
  0.0 0.8 compare_select_fusion
  0.8 23.6 %all_to_all.30 = bf16[8,64,128]{2,1,0:T(8,128)(2,1)S(1)} all-to-all(bf16[8,64,128]{2,1,0:T(8,128)(2,1)S(1)} %broadcast_in_dim.23), channel_id=1, replica_groups=mesh['y'=4,'zh'=2,'core'=2,'x'=4,'zl'=8] {'zl'}, dimensions={0} | all-to-all | bytes 262144 | tf_op jit(solution)/shard_map/all_to_all | solution.py:39
  24.4 0.1 broadcast_in_dim.24
  24.5 0.0 copy-start
  24.5 12.2 %all_to_all.31 = bf16[4,512,128]{2,1,0:T(8,128)(2,1)S(1)} all-to-all(bf16[4,512,128]{2,1,0:T(8,128)(2,1)S(1)} %broadcast_in_dim.24), channel_id=1, replica_groups=mesh['y'=4,'zh'=2,'core'=2,'x'=4,'zl'=8] {'x'}, dimensions={0} | all-to-all | bytes 1048576 | tf_op jit(solution)/shard_map/all_to_all | solution.py:39
  36.7 2.9 %convolution_bitcast_fusion = f32[16,8,8,128]{3,2,1,0:T(8,128)S(1)} fusion(bf16[2048,128]{1,0:T(8,128)(2,1)S(1)} %bitcast.29, bf16[2048,1024]{1,0:T(8,128)(2,1)} %param.9), kind=kOutput, calls=%fused_computation.1 | convolution fusion | flops 536870912 | bytes 5242880 | tf_op jit(solution)/shard_map/dot_general | solution.py:51
  39.6 0.8 copy.28
  40.4 4.5 %all-to-all-start.2 = ((f32[8,128,128]{1,2,0:T(8,128)}), f32[8,128,128]{1,2,0:T(8,128)S(1)}, u32[]{:S(2)}, u32[]{:S(2)}) async-start(f32[8,128,128]{1,2,0:T(8,128)} %bitcast.28), calls=%async_computation.2 | async-start | bytes 1048576 | tf_op jit(solution)/shard_map/all_to_all | solution.py:45
  44.9 0.8 dynamic_slice.3
  45.7 0.0 copy-done
  45.7 0.1 add_divide_fusion
  45.8 9.5 %all-to-all-done.2 = f32[8,128,128]{1,2,0:T(8,128)S(1)} async-done(((f32[8,128,128]{1,2,0:T(8,128)}), f32[8,128,128]{1,2,0:T(8,128)S(1)}, u32[]{:S(2)}, u32[]{:S(2)}) %all-to-all-start.2) | async-done | bytes 524320 | tf_op jit(solution)/shard_map/all_to_all | solution.py:45
  55.3 8.2 %collective-permute-start = (f32[128,128]{0,1:T(8,128)S(1)}, f32[128,128]{0,1:T(8,128)S(1)}, u32[]{:S(2)}, u32[]{:S(2)}) collective-permute-start(f32[128,128]{0,1:T(8,128)S(1)} %reduce_sum.27), channel_id=1, source_target_pairs={{0,64},{64,0},{1,65},{65,1},{2,66},{66,2},{3,67},{67,3},{4,68},{68... | collective-permute-start | bytes 196616 | tf_op jit(solution)/shard_map/ppermute | solution.py:53
  63.5 9.8 %collective-permute-done = f32[128,128]{0,1:T(8,128)S(1)} collective-permute-done((f32[128,128]{0,1:T(8,128)S(1)}, f32[128,128]{0,1:T(8,128)S(1)}, u32[]{:S(2)}, u32[]{:S(2)}) %collective-permute-start) | collective-permute-done | bytes 65568 | tf_op jit(solution)/shard_map/ppermute | solution.py:53
  73.3 0.4 convolution_multiply_fusion
  73.7 0.3 convolution_convert_fusion.1
  74.1 0.1 copy.16
  74.2 9.9 %all_to_all.32 = bf16[8,128,128]{2,1,0:T(8,128)(2,1)S(1)} all-to-all(bf16[8,128,128]{2,1,0:T(8,128)(2,1)S(1)} %broadcast_in_dim.27), channel_id=1, replica_groups=mesh['y'=4,'zh'=2,'core'=2,'x'=4,'zl'=8] {'y','core'}, dimensions={0} | all-to-all | bytes 524288 | tf_op jit(solution)/shard_map/all_to_all | solution.py:39
  84.2 3.7 %convolution_convert_fusion = bf16[128,2048]{1,0:T(8,128)(2,1)S(1)} fusion(bf16[1024,128]{1,0:T(8,128)(2,1)S(1)} %bitcast.32, bf16[2048,1024]{1,0:T(8,128)(2,1)} %param.9), kind=kOutput, calls=%fused_computation | convolution fusion | flops 537133056 | bytes 4980736 | tf_op jit(solution)/shard_map/dot_general | solution.py:57
  87.9 11.8 %all_to_all.33 = bf16[4,512,128]{1,2,0:T(8,128)(2,1)S(1)} all-to-all(bf16[4,512,128]{1,2,0:T(8,128)(2,1)S(1)} %bitcast.31), channel_id=1, replica_groups=mesh['y'=4,'zh'=2,'core'=2,'x'=4,'zl'=8] {'x'}, dimensions={0} | all-to-all | bytes 1048576 | tf_op jit(solution)/shard_map/all_to_all | solution.py:45
  99.7 0.1 convert_reduce_fusion
  99.8 0.1 copy.19
  99.9 18.8 %all_to_all.34 = f32[8,64,128]{2,1,0:T(8,128)S(1)} all-to-all(f32[8,64,128]{2,1,0:T(8,128)S(1)} %bitcast.33), channel_id=1, replica_groups=mesh['y'=4,'zh'=2,'core'=2,'x'=4,'zl'=8] {'zl'}, dimensions={0} | all-to-all | bytes 524288 | tf_op jit(solution)/shard_map/all_to_all | solution.py:45
  118.7 0.6 reduce_sum.29
  (6 shorter events, 0.1 us)
Async XLA Ops:
  24.5 21.2 %copy-start = (f32[32]{0:T(128)S(1)}, f32[32]{0:T(128)}, u32[]{:S(2)}) copy-start(f32[32]{0:T(128)} %param.11) | copy-start | bytes 388
  40.4 14.8 %all-to-all-start.2 = ((f32[8,128,128]{1,2,0:T(8,128)}), f32[8,128,128]{1,2,0:T(8,128)S(1)}, u32[]{:S(2)}, u32[]{:S(2)}) async-start(f32[8,128,128]{1,2,0:T(8,128)} %bitcast.28), calls=%async_computation.2 | async-start | bytes 1048576 | tf_op jit(solution)/shard_map/all_to_all | solution.py:45
  55.3 18.0 %collective-permute-start = (f32[128,128]{0,1:T(8,128)S(1)}, f32[128,128]{0,1:T(8,128)S(1)}, u32[]{:S(2)}, u32[]{:S(2)}) collective-permute-start(f32[128,128]{0,1:T(8,128)S(1)} %reduce_sum.27), channel_id=1, source_target_pairs={{0,64},{64,0},{1,65},{65,1},{2,66},{66,2},{3,67},{67,3},{4,68},{68... | collective-permute-start | bytes 196616 | tf_op jit(solution)/shard_map/ppermute | solution.py:53

commit v2 on v1

v2 whole, which is shorter than its diff:
```python
import math

import jax
import jax.numpy as jnp
import numpy as np
from jax import lax
from jax.experimental import pallas as pl
from jax.experimental.pallas import tpu as pltpu
from jax.sharding import Mesh
from jax.sharding import PartitionSpec as P

MONTHS = 32
VARS = 4
COLS = MONTHS * VARS
ROW = ("y", "zh", "core")
COL = ("x", "zl")
EXTRA = 8
TOP = 14
VMEM = pl.BlockSpec(memory_space=pltpu.VMEM)
ANY = pl.BlockSpec(memory_space=pl.ANY)


def cosine_blocks():
    freq = np.arange(MONTHS)[:, None]
    month = np.arange(MONTHS)[None, :]
    table = np.cos(math.pi * (month + 0.5) * freq / MONTHS) * math.sqrt(2.0 / MONTHS)
    table[0] /= math.sqrt(2.0)
    return np.kron(np.eye(VARS), table).astype(np.float32)


def kernel_call(body, out_shape, in_specs, flops, nbytes, scratch_shapes=()):
    return pl.pallas_call(
        body,
        out_shape=out_shape,
        in_specs=in_specs,
        out_specs=VMEM,
        scratch_shapes=scratch_shapes,
        compiler_params=pltpu.CompilerParams(vmem_limit_bytes=12 * 2**20),
        cost_estimate=pl.CostEstimate(flops=flops, bytes_accessed=nbytes, transcendentals=0),
    )


def fetched(source, held, sem):
    copy = pltpu.make_async_copy(source, held, sem)
    copy.start()
    copy.wait()
    return held[...]


def scaled(values):
    largest = jnp.maximum(jnp.max(jnp.abs(values), keepdims=True), 1e-30)
    exponent = jnp.floor(jnp.log(largest) * (1 / math.log(2.0))) - TOP
    return values * jnp.exp2(-exponent), exponent


def put_exponent(out, exponent):
    rows = out.shape[1] - EXTRA
    out[:, rows:, :] = jnp.broadcast_to(exponent.reshape(1, 1, 1), (out.shape[0], EXTRA, out.shape[2]))


def split_kernel(proj, out):
    proj, exponent = scaled(proj[...])
    size = out.shape[2]
    for piece in range(out.shape[0]):
        out[piece, :COLS, :] = proj[:, piece * size : (piece + 1) * size]
    put_exponent(out, exponent)


def pair_kernel(pair, out):
    total, exponent = scaled(pair[0] + pair[1])
    out[0, :COLS, :] = total
    put_exponent(out, exponent)


def shrink_kernel(halves, table, lam_space, lam_time, out):
    total = sum(halves[half, :COLS, :] * jnp.exp2(halves[half, COLS : COLS + 1, :]) for half in range(halves.shape[0]))
    diagonal = lax.broadcasted_iota(jnp.int32, (MONTHS, MONTHS), 0) == lax.broadcasted_iota(jnp.int32, (MONTHS, MONTHS), 1)
    time = jnp.sum(jnp.where(diagonal, lam_time[...], 0.0), axis=1, keepdims=True)
    lines = total.shape[1] // lam_space.shape[1]
    space = [lam_space[pl.ds(lax.axis_index("y") * lines + line, 1), :] for line in range(lines)]
    gain = jnp.concatenate([time] * VARS, axis=0) * jnp.concatenate(space, axis=1)
    gain = gain / (gain + 1.0)
    spec = jnp.dot(table[...], total, precision=lax.Precision.HIGHEST, preferred_element_type=jnp.float32)
    back = lax.dot_general(
        spec * gain,
        table[...],
        (((0,), (0,)), ((), ())),
        precision=lax.Precision.HIGHEST,
        preferred_element_type=jnp.float32,
    )
    out[...] = back.astype(jnp.bfloat16)


def smooth_kernel(eigvec, coeffs, out, held, sem):
    out[...] = jnp.dot(fetched(eigvec, held, sem), coeffs[...], preferred_element_type=jnp.float32).astype(jnp.bfloat16)


def join_kernel(parts, out):
    total = parts[0].astype(jnp.float32)
    for peer in range(1, parts.shape[0]):
        total = total + parts[peer].astype(jnp.float32)
    total, exponent = scaled(total)
    size = out.shape[1] - EXTRA
    for piece in range(out.shape[0]):
        out[piece, :size, :] = total[piece * size : (piece + 1) * size]
    put_exponent(out, exponent)


def gather(block, axes):
    size = lax.axis_size(axes)
    copies = jnp.broadcast_to(block, (size,) + block.shape)
    return lax.all_to_all(copies, axes, 0, 0).reshape((size * block.shape[0],) + block.shape[1:])


def exchange_sum(pieces, axes):
    got = lax.all_to_all(pieces.astype(jnp.float16), axes, 0, 0).astype(jnp.float32)
    rows = got.shape[1] - EXTRA
    return (got[:, :rows] * jnp.exp2(got[:, rows : rows + 1])).sum(0)


def shards(observed, prior_mean, missing, eigvec, lam_space, lam_time):
    stations, eigs = eigvec.shape
    pieces = lax.axis_size("y")
    share = eigs // pieces
    flops = 2 * stations * eigs * COLS
    nbytes = 2 * stations * eigs
    filled = jnp.where(missing == 1, prior_mean, observed)
    filled = gather(gather(filled, "zl"), "x")
    proj = lax.dot_general(filled, eigvec, (((0,), (0,)), ((), ())), preferred_element_type=jnp.float32)
    split = kernel_call(
        split_kernel, jax.ShapeDtypeStruct((pieces, COLS + EXTRA, share), jnp.float32), [VMEM], eigs * COLS, 8 * eigs * COLS
    )(proj)
    pair = lax.all_gather(exchange_sum(split, "y"), "core")
    half = kernel_call(
        pair_kernel, jax.ShapeDtypeStruct((1, COLS + EXTRA, share), jnp.float32), [VMEM], share * COLS, 12 * share * COLS
    )(pair)
    halves = lax.all_gather(half.astype(jnp.float16), "zh", axis=0, tiled=True).astype(jnp.float32)
    coeffs = kernel_call(
        shrink_kernel, jax.ShapeDtypeStruct((share, COLS), jnp.bfloat16), [VMEM] * 4, 4 * COLS * COLS * share, COLS * COLS * 8
    )(halves, cosine_blocks(), lam_space.reshape(-1, COLS), lam_time.reshape(1, MONTHS))
    scratch = [pltpu.VMEM(eigvec.shape, eigvec.dtype), pltpu.SemaphoreType.DMA]
    part = kernel_call(
        smooth_kernel, jax.ShapeDtypeStruct((stations, COLS), jnp.bfloat16), [ANY, VMEM], flops, nbytes, scratch
    )(eigvec, gather(coeffs, "y"))
    across, along = lax.axis_size("x"), lax.axis_size("zl")
    parts = lax.all_to_all(part.reshape(across, stations // across, COLS), "x", 0, 0)
    joined = kernel_call(
        join_kernel,
        jax.ShapeDtypeStruct((along, stations // across // along + EXTRA, COLS), jnp.float32),
        [VMEM],
        stations * COLS,
        4 * stations * COLS,
    )(parts)
    return exchange_sum(joined, "zl")


def solution(mesh):
    fine = Mesh(mesh.devices.reshape(4, 2, 2, 4, 8), ("y", "zh", "core", "x", "zl"))
    rows = P(ROW + COL, None)
    in_specs = (rows, rows, rows, P(ROW, COL), P(COL), P())
    return jax.shard_map(shards, mesh=fine, in_specs=in_specs, out_specs=rows, check_vma=False)
```

time: 120 us -> 110 us (0.917)
  the two profiles are of different devices: /device:TPU:32 before, /device:TPU:2 now
where the time goes in v2:
time: 110 us; the launch traced here: 109 us
  blocking collectives  101 us (92%)
  matrix products  2.96 us (3%)
  Pallas kernels  2.83 us (3%)
  other arithmetic  1.66 us (2%)
    all_to_all x3, blocking collectives, gather(): lax.all_to_all(copies, axes, 0, 0)  44.6 us
    all_to_all x2, blocking collectives, exchange_sum(): lax.all_to_all(pieces.astype(jnp.float16), axes, 0, 0).astype(jnp.float32)  26.9 us
    all_gather x1, blocking collectives, shards(): lax.all_gather(half.astype(jnp.float16), 'zh', axis=0, tiled=True)  17.4 us
    all_to_all x1, blocking collectives, shards(): lax.all_to_all(part.reshape(across, stations // across, COLS), 'x', 0, 0)  10.5 us
    dot_general x1, matrix products, shards(): lax.dot_general(filled, eigvec, (((0,), (0,)), ((), ())), preferred_eleme...  2.96 us

profile of v2, /device:TPU:2, one launch (start us, length us, event | category | flops | bytes accessed | tf_op | source)
XLA Modules:
  0.0 109.1 jit_solution(2019065239326369848)
XLA Ops:
  0.0 0.8 compare_select_fusion
  0.8 24.3 %all_to_all.30 = bf16[8,64,128]{2,1,0:T(8,128)(2,1)S(1)} all-to-all(bf16[8,64,128]{2,1,0:T(8,128)(2,1)S(1)} %broadcast_in_dim.9), channel_id=1, replica_groups=mesh['y'=4,'zh'=2,'core'=2,'x'=4,'zl'=8] {'zl'}, dimensions={0} | all-to-all | bytes 262144 | tf_op jit(solution)/shard_map/all_to_all | solution.py:112
  25.1 0.1 broadcast_in_dim.10
  25.2 11.3 %all_to_all.31 = bf16[4,512,128]{2,1,0:T(8,128)(2,1)S(1)} all-to-all(bf16[4,512,128]{2,1,0:T(8,128)(2,1)S(1)} %broadcast_in_dim.10), channel_id=1, replica_groups=mesh['y'=4,'zh'=2,'core'=2,'x'=4,'zl'=8] {'x'}, dimensions={0} | all-to-all | bytes 1048576 | tf_op jit(solution)/shard_map/all_to_all | solution.py:112
  36.4 0.0 copy-start.1
  36.4 0.0 copy-start.2
  36.4 0.0 copy-start.3
  36.4 3.0 %fusion.4.proj = f32[128,1024]{1,0:T(8,128)S(1)} fusion(bf16[2048,128]{1,0:T(8,128)(2,1)S(1)} %bitcast.18, bf16[2048,1024]{1,0:T(8,128)(2,1)} %eigvec.1), kind=kOutput, calls=%fused_computation.10 | convolution fusion | flops 536870912 | bytes 5242880 | tf_op jit(solution)/shard_map/dot_general | solution.py:129
  39.4 0.0 copy-start
  39.4 0.2 shard_map.73
  39.7 11.3 %all_to_all.32 = f16[4,136,256]{2,1,0:T(8,128)(2,1)S(1)} all-to-all(f16[4,136,256]{2,1,0:T(8,128)(2,1)S(1)} %convert_element_type.18), channel_id=1, replica_groups=mesh['y'=4,'zh'=2,'core'=2,'x'=4,'zl'=8] {'y'}, dimensions={0} | all-to-all | bytes 557056 | tf_op jit(solution)/shard_map/all_to_all | solution.py:116
  51.1 2.0 %all-gather = f32[256,256]{1,0:T(8,128)S(1)} all-gather(f32[128,256]{1,0:T(8,128)S(1)} %fusion), channel_id=2, replica_groups=mesh['y'=4,'zh'=2,'core'=2,'x'=4,'zl'=8] {'core'}, dimensions={0}, use_global_device_ids=true | all-gather | bytes 393216 | tf_op jit(solution)/shard_map/all_gather | solution.py:133
  53.1 0.2 shard_map.74
  53.3 17.4 %all_gather.11 = f16[2,136,256]{2,1,0:T(8,128)(2,1)S(1)} all-gather(f16[1,136,256]{2,1,0:T(8,128)(2,1)S(1)} %convert_element_type.20), channel_id=1, replica_groups=mesh['y'=4,'zh'=2,'core'=2,'x'=4,'zl'=8] {'zh'}, dimensions={0}, use_global_device_ids=true | all-gather | bytes 208896 | tf_op jit(solution)/shard_map/all_gather | solution.py:137
  70.7 0.0 copy-done.1
  70.7 0.0 copy-done.2
  70.7 0.0 copy-done.3
  70.7 0.7 shard_map.75
  71.5 9.1 %all_to_all.33 = bf16[4,256,128]{2,1,0:T(8,128)(2,1)S(1)} all-to-all(bf16[4,256,128]{2,1,0:T(8,128)(2,1)S(1)} %broadcast_in_dim.11), channel_id=1, replica_groups=mesh['y'=4,'zh'=2,'core'=2,'x'=4,'zl'=8] {'y'}, dimensions={0} | all-to-all | bytes 524288 | tf_op jit(solution)/shard_map/all_to_all | solution.py:112
  80.6 0.0 copy-done
  80.6 1.5 %shard_map.76 = bf16[2048,128]{1,0:T(8,128)(2,1)S(1)} custom-call(bf16[2048,1024]{1,0:T(8,128)(2,1)S(1)} %copy-done, bf16[1024,128]{1,0:T(8,128)(2,1)S(1)} %bitcast.14), custom_call_target="tpu_custom_call" | custom-call | flops 536870912 | bytes 4194304 | tf_op jit(solution)/shard_map/pallas_call | solution.py:142
  82.1 10.5 %all_to_all.34.parts = bf16[4,512,128]{2,1,0:T(8,128)(2,1)S(1)} all-to-all(bf16[4,512,128]{2,1,0:T(8,128)(2,1)S(1)} %bitcast.13), channel_id=1, replica_groups=mesh['y'=4,'zh'=2,'core'=2,'x'=4,'zl'=8] {'x'}, dimensions={0} | all-to-all | bytes 1048576 | tf_op jit(solution)/shard_map/all_to_all | solution.py:146
  92.6 0.2 shard_map.77
  92.8 15.6 %all_to_all.35 = f16[8,72,128]{2,1,0:T(8,128)(2,1)S(1)} all-to-all(f16[8,72,128]{2,1,0:T(8,128)(2,1)S(1)} %convert_element_type.22), channel_id=1, replica_groups=mesh['y'=4,'zh'=2,'core'=2,'x'=4,'zl'=8] {'zl'}, dimensions={0} | all-to-all | bytes 294912 | tf_op jit(solution)/shard_map/all_to_all | solution.py:116
  108.5 0.6 fusion.1
  (12 shorter events, 0.3 us)
Async XLA Ops:
  36.4 34.3 %copy-start.1 = (f32[128,128]{1,0:T(8,128)S(1)}, f32[128,128]{1,0:T(8,128)}, u32[]{:S(2)}) copy-start(f32[128,128]{1,0:T(8,128)} %constant.3.clone.table) | copy-start | bytes 196612
  36.4 34.3 %copy-start.2 = (f32[1024]{0:T(1024)S(1)}, f32[1024]{0:T(1024)}, u32[]{:S(2)}) copy-start(f32[1024]{0:T(1024)} %param.11) | copy-start | bytes 12292
  36.4 34.3 %copy-start.3 = (f32[32]{0:T(128)S(1)}, f32[32]{0:T(128)}, u32[]{:S(2)}) copy-start(f32[32]{0:T(128)} %param.12) | copy-start | bytes 388
  39.4 41.2 %copy-start = (bf16[2048,1024]{1,0:T(8,128)(2,1)S(1)}, bf16[2048,1024]{1,0:T(8,128)(2,1)}, u32[]{:S(2)}) copy-start(bf16[2048,1024]{1,0:T(8,128)(2,1)} %eigvec.1) | copy-start | bytes 12582916

commit v3 on v2

--- a/solution.py
+++ b/solution.py
@@ -14,6 +14,7 @@
 COLS = MONTHS * VARS
 ROW = ("y", "zh", "core")
 COL = ("x", "zl")
+PAIR = ("y", "core")
 EXTRA = 8
 TOP = 14
 VMEM = pl.BlockSpec(memory_space=pltpu.VMEM)
@@ -66,18 +67,12 @@
     put_exponent(out, exponent)
 
 
-def pair_kernel(pair, out):
-    total, exponent = scaled(pair[0] + pair[1])
-    out[0, :COLS, :] = total
-    put_exponent(out, exponent)
-
-
 def shrink_kernel(halves, table, lam_space, lam_time, out):
     total = sum(halves[half, :COLS, :] * jnp.exp2(halves[half, COLS : COLS + 1, :]) for half in range(halves.shape[0]))
     diagonal = lax.broadcasted_iota(jnp.int32, (MONTHS, MONTHS), 0) == lax.broadcasted_iota(jnp.int32, (MONTHS, MONTHS), 1)
     time = jnp.sum(jnp.where(diagonal, lam_time[...], 0.0), axis=1, keepdims=True)
     lines = total.shape[1] // lam_space.shape[1]
-    space = [lam_space[pl.ds(lax.axis_index("y") * lines + line, 1), :] for line in range(lines)]
+    space = [lam_space[pl.ds(lax.axis_index(PAIR) * lines + line, 1), :] for line in range(lines)]
     gain = jnp.concatenate([time] * VARS, axis=0) * jnp.concatenate(space, axis=1)
     gain = gain / (gain + 1.0)
     spec = jnp.dot(table[...], total, precision=lax.Precision.HIGHEST, preferred_element_type=jnp.float32)
@@ -92,17 +87,10 @@
 
 
 def smooth_kernel(eigvec, coeffs, out, held, sem):
-    out[...] = jnp.dot(fetched(eigvec, held, sem), coeffs[...], preferred_element_type=jnp.float32).astype(jnp.bfloat16)
-
-
-def join_kernel(parts, out):
-    total = parts[0].astype(jnp.float32)
-    for peer in range(1, parts.shape[0]):
-        total = total + parts[peer].astype(jnp.float32)
-    total, exponent = scaled(total)
+    part, exponent = scaled(jnp.dot(fetched(eigvec, held, sem), coeffs[...], preferred_element_type=jnp.float32))
     size = out.shape[1] - EXTRA
     for piece in range(out.shape[0]):
-        out[piece, :size, :] = total[piece * size : (piece + 1) * size]
+        out[piece, :size, :] = part[piece * size : (piece + 1) * size]
     put_exponent(out, exponent)
 
 
@@ -112,15 +100,15 @@
     return lax.all_to_all(copies, axes, 0, 0).reshape((size * block.shape[0],) + block.shape[1:])
 
 
-def exchange_sum(pieces, axes):
+def exchange(pieces, axes):
     got = lax.all_to_all(pieces.astype(jnp.float16), axes, 0, 0).astype(jnp.float32)
     rows = got.shape[1] - EXTRA
-    return (got[:, :rows] * jnp.exp2(got[:, rows : rows + 1])).sum(0)
+    return got[:, :rows], got[:, rows : rows + 1]
 
 
 def shards(observed, prior_mean, missing, eigvec, lam_space, lam_time):
     stations, eigs = eigvec.shape
-    pieces = lax.axis_size("y")
+    pieces = lax.axis_size(PAIR)
     share = eigs // pieces
     flops = 2 * stations * eigs * COLS
     nbytes = 2 * stations * eigs
@@ -130,28 +118,26 @@
     split = kernel_call(
         split_kernel, jax.ShapeDtypeStruct((pieces, COLS + EXTRA, share), jnp.float32), [VMEM], eigs * COLS, 8 * eigs * COLS
     )(proj)
-    pair = lax.all_gather(exchange_sum(split, "y"), "core")
-    half = kernel_call(
-        pair_kernel, jax.ShapeDtypeStruct((1, COLS + EXTRA, share), jnp.float32), [VMEM], share * COLS, 12 * share * COLS
-    )(pair)
-    halves = lax.all_gather(half.astype(jnp.float16), "zh", axis=0, tiled=True).astype(jnp.float32)
+    terms, exponents = exchange(split, PAIR)
+    top = exponents.max(0) + math.log2(pieces)
+    half = jnp.concatenate([(terms * jnp.exp2(exponents - top)).sum(0), jnp.broadcast_to(top, (EXTRA, share))])
+    halves = lax.all_gather(half.astype(jnp.float16), "zh").astype(jnp.float32)
     coeffs = kernel_call(
         shrink_kernel, jax.ShapeDtypeStruct((share, COLS), jnp.bfloat16), [VMEM] * 4, 4 * COLS * COLS * share, COLS * COLS * 8
     )(halves, cosine_blocks(), lam_space.reshape(-1, COLS), lam_time.reshape(1, MONTHS))
     scratch = [pltpu.VMEM(eigvec.shape, eigvec.dtype), pltpu.SemaphoreType.DMA]
+    across, along = lax.axis_size("x"), lax.axis_size("zl")
     part = kernel_call(
-        smooth_kernel, jax.ShapeDtypeStruct((stations, COLS), jnp.bfloat16), [ANY, VMEM], flops, nbytes, scratch
-    )(eigvec, gather(coeffs, "y"))
-    across, along = lax.axis_size("x"), lax.axis_size("zl")
-    parts = lax.all_to_all(part.reshape(across, stations // across, COLS), "x", 0, 0)
-    joined = kernel_call(
-        join_kernel,
-        jax.ShapeDtypeStruct((along, stations // across // along + EXTRA, COLS), jnp.float32),
-        [VMEM],
-        stations * COLS,
-        4 * stations * COLS,
-    )(parts)
-    return exchange_sum(joined, "zl")
+        smooth_kernel,
+        jax.ShapeDtypeStruct((across, stations // across + EXTRA, COLS), jnp.float32),
+        [ANY, VMEM],
+        flops,
+        nbytes,
+        scratch,
+    )(eigvec, gather(coeffs, PAIR))
+    terms, exponents = exchange(part, "x")
+    joined = (terms * jnp.exp2(exponents)).sum(0).astype(jnp.bfloat16).reshape(along, -1, COLS)
+    return lax.all_to_all(joined, "zl", 0, 0).astype(jnp.float32).sum(0)
 
 
 def solution(mesh):

time: 110 us -> 107 us (0.973)
  blocking collectives: 101 us -> 99.3 us
    all_gather x2 -> x1, blocking collectives: 19.4 us -> 13.3 us  [shards(): halves = lax.all_gather(half.astype(jnp.float16), 'zh').astype(jnp.float32)]
    all_to_all x3, blocking collectives: 37.4 us -> 40 us  [the longest x2 23.9 us: exchange(): lax.all_to_all(pieces.astype(jnp.float16), axes, 0, 0).astype(jnp.float32)]
    all_to_all x3, blocking collectives: 44.6 us -> 46 us  [gather(): lax.all_to_all(copies, axes, 0, 0)]
where the time goes in v3:
time: 107 us
  blocking collectives  99.3 us (93%)
  matrix products  3.07 us (3%)
  Pallas kernels  2.48 us (2%)
  other arithmetic  1.86 us (2%)
    all_to_all x3, blocking collectives, gather(): lax.all_to_all(copies, axes, 0, 0)  46 us
    all_to_all x2, blocking collectives, exchange(): lax.all_to_all(pieces.astype(jnp.float16), axes, 0, 0).astype(jnp.float32)  23.9 us
    all_to_all x1, blocking collectives, shards(): return lax.all_to_all(joined, 'zl', 0, 0).astype(jnp.float32).sum(0)  16.1 us
    all_gather x1, blocking collectives, shards(): halves = lax.all_gather(half.astype(jnp.float16), 'zh').astype(jnp.float32)  13.3 us
    dot_general x1, matrix products, shards(): lax.dot_general(filled, eigvec, (((0,), (0,)), ((), ())), preferred_eleme...  3.07 us

profile of v3, /device:TPU:2, one launch (start us, length us, event | category | flops | bytes accessed | tf_op | source)
XLA Modules:
  0.0 107.0 jit_solution(1797784292200369862)
XLA Ops:
  0.0 0.8 compare_select_fusion
  0.8 24.3 %all_to_all.30 = bf16[8,64,128]{2,1,0:T(8,128)(2,1)S(1)} all-to-all(bf16[8,64,128]{2,1,0:T(8,128)(2,1)S(1)} %broadcast_in_dim.15), channel_id=1, replica_groups=mesh['y'=4,'zh'=2,'core'=2,'x'=4,'zl'=8] {'zl'}, dimensions={0} | all-to-all | bytes 262144 | tf_op jit(solution)/shard_map/all_to_all | solution.py:100
  25.1 0.1 broadcast_in_dim.16
  25.2 11.3 %all_to_all.31 = bf16[4,512,128]{2,1,0:T(8,128)(2,1)S(1)} all-to-all(bf16[4,512,128]{2,1,0:T(8,128)(2,1)S(1)} %broadcast_in_dim.16), channel_id=1, replica_groups=mesh['y'=4,'zh'=2,'core'=2,'x'=4,'zl'=8] {'x'}, dimensions={0} | all-to-all | bytes 1048576 | tf_op jit(solution)/shard_map/all_to_all | solution.py:100
  36.4 0.0 copy-start.1
  36.4 0.0 copy-start.2
  36.4 0.0 copy-start.3
  36.4 0.0 copy-start
  36.4 3.1 %fusion.4.proj = f32[128,1024]{1,0:T(8,128)S(1)} fusion(bf16[2048,128]{1,0:T(8,128)(2,1)S(1)} %bitcast.15, bf16[2048,1024]{1,0:T(8,128)(2,1)} %eigvec.1), kind=kOutput, calls=%fused_computation.14 | convolution fusion | flops 536870912 | bytes 5242880 | tf_op jit(solution)/shard_map/dot_general | solution.py:117
  39.5 0.2 shard_map.73
  39.8 12.0 %all_to_all.32 = f16[8,136,128]{2,1,0:T(8,128)(2,1)S(1)} all-to-all(f16[8,136,128]{2,1,0:T(8,128)(2,1)S(1)} %convert_element_type.33), channel_id=1, replica_groups=mesh['y'=4,'zh'=2,'core'=2,'x'=4,'zl'=8] {'y','core'}, dimensions={0} | all-to-all | bytes 557056 | tf_op jit(solution)/shard_map/all_to_all | solution.py:104
  51.9 13.3 %all_gather.4 = f16[2,136,128]{2,1,0:T(8,128)(2,1)S(1)} all-gather(f16[1,136,128]{2,1,0:T(8,128)(2,1)S(1)} %pad_maximum_fusion), channel_id=1, replica_groups=mesh['y'=4,'zh'=2,'core'=2,'x'=4,'zl'=8] {'zh'}, dimensions={0}, use_global_device_ids=true | all-gather | bytes 104448 | tf_op jit(solution)/shard_map/all_gather | solution.py:124
  65.3 0.0 copy-done.1
  65.3 0.0 copy-done.2
  65.3 0.0 copy-done.3
  65.3 0.5 shard_map.74
  65.9 10.5 %all_to_all.33 = bf16[8,128,128]{2,1,0:T(8,128)(2,1)S(1)} all-to-all(bf16[8,128,128]{2,1,0:T(8,128)(2,1)S(1)} %broadcast_in_dim.18), channel_id=1, replica_groups=mesh['y'=4,'zh'=2,'core'=2,'x'=4,'zl'=8] {'y','core'}, dimensions={0} | all-to-all | bytes 524288 | tf_op jit(solution)/shard_map/all_to_all | solution.py:100
  76.4 0.0 copy-done
  76.4 1.7 %shard_map.75 = f32[4,520,128]{2,1,0:T(8,128)S(1)} custom-call(bf16[2048,1024]{1,0:T(8,128)(2,1)S(1)} %copy-done, bf16[1024,128]{1,0:T(8,128)(2,1)S(1)} %bitcast.12), custom_call_target="tpu_custom_call" | custom-call | flops 536870912 | bytes 4194304 | tf_op jit(solution)/shard_map/pallas_call | solution.py:130
  78.1 0.1 convert_element_type.36
  78.2 11.9 %all_to_all.34 = f16[4,520,128]{2,1,0:T(8,128)(2,1)S(1)} all-to-all(f16[4,520,128]{2,1,0:T(8,128)(2,1)S(1)} %convert_element_type.36), channel_id=1, replica_groups=mesh['y'=4,'zh'=2,'core'=2,'x'=4,'zl'=8] {'x'}, dimensions={0} | all-to-all | bytes 1064960 | tf_op jit(solution)/shard_map/all_to_all | solution.py:104
  90.1 0.1 convert_element_type.37
  90.2 0.1 fusion
  90.3 16.1 %all_to_all.35 = bf16[8,64,128]{2,1,0:T(8,128)(2,1)S(1)} all-to-all(bf16[8,64,128]{2,1,0:T(8,128)(2,1)S(1)} %bitcast.16), channel_id=1, replica_groups=mesh['y'=4,'zh'=2,'core'=2,'x'=4,'zl'=8] {'zl'}, dimensions={0} | all-to-all | bytes 262144 | tf_op jit(solution)/shard_map/all_to_all | solution.py:140
  106.4 0.6 convert_reduce_fusion
  (13 shorter events, 0.3 us)
Async XLA Ops:
  36.4 28.9 %copy-start.1 = (f32[128,128]{1,0:T(8,128)S(1)}, f32[128,128]{1,0:T(8,128)}, u32[]{:S(2)}) copy-start(f32[128,128]{1,0:T(8,128)} %constant.5.clone.table) | copy-start | bytes 196612
  36.4 28.9 %copy-start.2 = (f32[1024]{0:T(1024)S(1)}, f32[1024]{0:T(1024)}, u32[]{:S(2)}) copy-start(f32[1024]{0:T(1024)} %param.11) | copy-start | bytes 12292
  36.4 28.9 %copy-start.3 = (f32[32]{0:T(128)S(1)}, f32[32]{0:T(128)}, u32[]{:S(2)}) copy-start(f32[32]{0:T(128)} %param.12) | copy-start | bytes 388
  36.4 40.0 %copy-start = (bf16[2048,1024]{1,0:T(8,128)(2,1)S(1)}, bf16[2048,1024]{1,0:T(8,128)(2,1)}, u32[]{:S(2)}) copy-start(bf16[2048,1024]{1,0:T(8,128)(2,1)} %eigvec.1) | copy-start | bytes 12582916

commit v4 on v3

--- a/solution.py
+++ b/solution.py
@@ -1,3 +1,4 @@
+import functools
 import math
 
 import jax
@@ -13,7 +14,8 @@
 VARS = 4
 COLS = MONTHS * VARS
 ROW = ("y", "zh", "core")
-COL = ("x", "zl")
+COL = ("x", "za", "zc")
+NEAR = ("x", "zc")
 PAIR = ("y", "core")
 EXTRA = 8
 TOP = 14
@@ -86,11 +88,13 @@
     out[...] = back.astype(jnp.bfloat16)
 
 
-def smooth_kernel(eigvec, coeffs, out, held, sem):
+def smooth_kernel(far, eigvec, coeffs, out, held, sem):
     part, exponent = scaled(jnp.dot(fetched(eigvec, held, sem), coeffs[...], preferred_element_type=jnp.float32))
-    size = out.shape[1] - EXTRA
-    for piece in range(out.shape[0]):
-        out[piece, :size, :] = part[piece * size : (piece + 1) * size]
+    size = part.shape[0] // (out.shape[0] * far)
+    for block in range(part.shape[0] // size):
+        piece = block // (2 * far) * 2 + block % 2
+        start = block // 2 % far * size
+        out[piece, start : start + size, :] = part[block * size : (block + 1) * size]
     put_exponent(out, exponent)
 
 
@@ -113,7 +117,9 @@
     flops = 2 * stations * eigs * COLS
     nbytes = 2 * stations * eigs
     filled = jnp.where(missing == 1, prior_mean, observed)
-    filled = gather(gather(filled, "zl"), "x")
+    across, far, near = lax.axis_size("x"), lax.axis_size("za"), lax.axis_size("zc")
+    filled = gather(gather(filled, "za"), NEAR).reshape(across, near, far, -1, COLS)
+    filled = filled.transpose(0, 2, 1, 3, 4).reshape(stations, COLS)
     proj = lax.dot_general(filled, eigvec, (((0,), (0,)), ((), ())), preferred_element_type=jnp.float32)
     split = kernel_call(
         split_kernel, jax.ShapeDtypeStruct((pieces, COLS + EXTRA, share), jnp.float32), [VMEM], eigs * COLS, 8 * eigs * COLS
@@ -126,22 +132,21 @@
         shrink_kernel, jax.ShapeDtypeStruct((share, COLS), jnp.bfloat16), [VMEM] * 4, 4 * COLS * COLS * share, COLS * COLS * 8
     )(halves, cosine_blocks(), lam_space.reshape(-1, COLS), lam_time.reshape(1, MONTHS))
     scratch = [pltpu.VMEM(eigvec.shape, eigvec.dtype), pltpu.SemaphoreType.DMA]
-    across, along = lax.axis_size("x"), lax.axis_size("zl")
     part = kernel_call(
-        smooth_kernel,
-        jax.ShapeDtypeStruct((across, stations // across + EXTRA, COLS), jnp.float32),
+        functools.partial(smooth_kernel, far),
+        jax.ShapeDtypeStruct((across * near, stations // (across * near) + EXTRA, COLS), jnp.float32),
         [ANY, VMEM],
         flops,
         nbytes,
         scratch,
     )(eigvec, gather(coeffs, PAIR))
-    terms, exponents = exchange(part, "x")
-    joined = (terms * jnp.exp2(exponents)).sum(0).astype(jnp.bfloat16).reshape(along, -1, COLS)
-    return lax.all_to_all(joined, "zl", 0, 0).astype(jnp.float32).sum(0)
+    terms, exponents = exchange(part, NEAR)
+    joined = (terms * jnp.exp2(exponents)).sum(0).astype(jnp.bfloat16).reshape(far, -1, COLS)
+    return lax.all_to_all(joined, "za", 0, 0).astype(jnp.float32).sum(0)
 
 
 def solution(mesh):
-    fine = Mesh(mesh.devices.reshape(4, 2, 2, 4, 8), ("y", "zh", "core", "x", "zl"))
+    fine = Mesh(mesh.devices.reshape(4, 2, 2, 4, 4, 2), ROW + COL)
     rows = P(ROW + COL, None)
     in_specs = (rows, rows, rows, P(ROW, COL), P(COL), P())
     return jax.shard_map(shards, mesh=fine, in_specs=in_specs, out_specs=rows, check_vma=False)

time: 107 us -> 104 us (0.972)
  blocking collectives: 99.3 us -> 96.3 us
    all_to_all x1, blocking collectives: 16.1 us -> 13.2 us  [shards(): return lax.all_to_all(joined, 'za', 0, 0).astype(jnp.float32).sum(0)]
    all_to_all x3, blocking collectives: 46 us -> 44.2 us  [gather(): lax.all_to_all(copies, axes, 0, 0)]
    all_to_all x2, blocking collectives: 23.9 us -> 25.5 us  [exchange(): lax.all_to_all(pieces.astype(jnp.float16), axes, 0, 0).astype(jnp.float32)]
where the time goes in v4:
time: 104 us
  blocking collectives  96.3 us (93%)
  matrix products  3.07 us (3%)
  Pallas kernels  2.49 us (2%)
  other arithmetic  1.86 us (2%)
    all_to_all x3, blocking collectives, gather(): lax.all_to_all(copies, axes, 0, 0)  44.2 us
    all_to_all x2, blocking collectives, exchange(): lax.all_to_all(pieces.astype(jnp.float16), axes, 0, 0).astype(jnp.float32)  25.5 us
    all_gather x1, blocking collectives, shards(): halves = lax.all_gather(half.astype(jnp.float16), 'zh').astype(jnp.float32)  13.3 us
    all_to_all x1, blocking collectives, shards(): return lax.all_to_all(joined, 'za', 0, 0).astype(jnp.float32).sum(0)  13.2 us
    dot_general x1, matrix products, shards(): lax.dot_general(filled, eigvec, (((0,), (0,)), ((), ())), preferred_eleme...  3.07 us

profile of v4, /device:TPU:2, one launch (start us, length us, event | category | flops | bytes accessed | tf_op | source)
XLA Modules:
  0.0 104.1 jit_solution(563625217819555749)
XLA Ops:
  0.0 0.8 compare_select_fusion
  0.8 21.1 %all_to_all.30 = bf16[4,64,128]{2,1,0:T(8,128)(2,1)S(1)} all-to-all(bf16[4,64,128]{2,1,0:T(8,128)(2,1)S(1)} %broadcast_in_dim.15), channel_id=1, replica_groups=mesh['y'=4,'zh'=2,'core'=2,'x'=4,'za'=4,'zc'=2] {'za'}, dimensions={0} | all-to-all | bytes 131072 | tf_op jit(solution)/shard_map/all_to_all | solution.py:104
  21.9 0.1 broadcast_in_dim.16
  22.0 12.7 %all_to_all.31 = bf16[8,256,128]{2,1,0:T(8,128)(2,1)S(1)} all-to-all(bf16[8,256,128]{2,1,0:T(8,128)(2,1)S(1)} %broadcast_in_dim.16), channel_id=1, replica_groups=mesh['y'=4,'zh'=2,'core'=2,'x'=4,'za'=4,'zc'=2] {'x','zc'}, dimensions={0} | all-to-all | bytes 1048576 | tf_op jit(solution)/shard_map/all_to_all | solution.py:104
  34.7 0.0 copy-start.1
  34.7 0.0 copy-start.2
  34.7 0.0 copy-start.3
  34.7 0.0 copy-start
  34.7 3.1 %fusion.4.proj = f32[128,1024]{1,0:T(8,128)S(1)} fusion(bf16[2048,128]{1,0:T(8,128)(2,1)S(1)} %bitcast.18, bf16[2048,1024]{1,0:T(8,128)(2,1)} %eigvec.1), kind=kOutput, calls=%fused_computation.14 | convolution fusion | flops 536870912 | bytes 5242880 | tf_op jit(solution)/shard_map/dot_general | solution.py:123
  37.8 0.2 shard_map.73
  38.1 12.0 %all_to_all.32 = f16[8,136,128]{2,1,0:T(8,128)(2,1)S(1)} all-to-all(f16[8,136,128]{2,1,0:T(8,128)(2,1)S(1)} %convert_element_type.33), channel_id=1, replica_groups=mesh['y'=4,'zh'=2,'core'=2,'x'=4,'za'=4,'zc'=2] {'y','core'}, dimensions={0} | all-to-all | bytes 557056 | tf_op jit(solution)/shard_map/all_to_all | solution.py:108
  50.2 13.3 %all_gather.4 = f16[2,136,128]{2,1,0:T(8,128)(2,1)S(1)} all-gather(f16[1,136,128]{2,1,0:T(8,128)(2,1)S(1)} %pad_maximum_fusion), channel_id=1, replica_groups=mesh['y'=4,'zh'=2,'core'=2,'x'=4,'za'=4,'zc'=2] {'zh'}, dimensions={0}, use_global_device_ids=true | all-gather | bytes 104448 | tf_op jit(solution)/shard_map/all_gather | solution.py:130
  63.6 0.0 copy-done.1
  63.6 0.0 copy-done.2
  63.6 0.0 copy-done.3
  63.6 0.5 shard_map.74
  64.2 10.5 %all_to_all.33 = bf16[8,128,128]{2,1,0:T(8,128)(2,1)S(1)} all-to-all(bf16[8,128,128]{2,1,0:T(8,128)(2,1)S(1)} %broadcast_in_dim.18), channel_id=1, replica_groups=mesh['y'=4,'zh'=2,'core'=2,'x'=4,'za'=4,'zc'=2] {'y','core'}, dimensions={0} | all-to-all | bytes 524288 | tf_op jit(solution)/shard_map/all_to_all | solution.py:104
  74.7 0.0 copy-done
  74.7 1.8 %shard_map.75 = f32[8,264,128]{2,1,0:T(8,128)S(1)} custom-call(bf16[2048,1024]{1,0:T(8,128)(2,1)S(1)} %copy-done, bf16[1024,128]{1,0:T(8,128)(2,1)S(1)} %bitcast.15), custom_call_target="tpu_custom_call" | custom-call | flops 536870912 | bytes 4194304 | tf_op jit(solution)/shard_map/pallas_call | solution.py:135
  76.5 0.1 convert_element_type.36
  76.5 13.5 %all_to_all.34 = f16[8,264,128]{2,1,0:T(8,128)(2,1)S(1)} all-to-all(f16[8,264,128]{2,1,0:T(8,128)(2,1)S(1)} %convert_element_type.36), channel_id=1, replica_groups=mesh['y'=4,'zh'=2,'core'=2,'x'=4,'za'=4,'zc'=2] {'x','zc'}, dimensions={0} | all-to-all | bytes 1081344 | tf_op jit(solution)/shard_map/all_to_all | solution.py:108
  90.0 0.1 convert_element_type.37
  90.1 0.1 fusion
  90.2 13.2 %all_to_all.35 = bf16[4,64,128]{2,1,0:T(8,128)(2,1)S(1)} all-to-all(bf16[4,64,128]{2,1,0:T(8,128)(2,1)S(1)} %bitcast.20), channel_id=1, replica_groups=mesh['y'=4,'zh'=2,'core'=2,'x'=4,'za'=4,'zc'=2] {'za'}, dimensions={0} | all-to-all | bytes 131072 | tf_op jit(solution)/shard_map/all_to_all | solution.py:145
  103.4 0.6 convert_reduce_fusion
  (14 shorter events, 0.3 us)
Async XLA Ops:
  34.7 28.9 %copy-start.1 = (f32[128,128]{1,0:T(8,128)S(1)}, f32[128,128]{1,0:T(8,128)}, u32[]{:S(2)}) copy-start(f32[128,128]{1,0:T(8,128)} %constant.12.clone.table) | copy-start | bytes 196612
  34.7 28.9 %copy-start.2 = (f32[1024]{0:T(1024)S(1)}, f32[1024]{0:T(1024)}, u32[]{:S(2)}) copy-start(f32[1024]{0:T(1024)} %param.11) | copy-start | bytes 12292
  34.7 28.9 %copy-start.3 = (f32[32]{0:T(128)S(1)}, f32[32]{0:T(128)}, u32[]{:S(2)}) copy-start(f32[32]{0:T(128)} %param.12) | copy-start | bytes 388
  34.7 40.0 %copy-start = (bf16[2048,1024]{1,0:T(8,128)(2,1)S(1)}, bf16[2048,1024]{1,0:T(8,128)(2,1)}, u32[]{:S(2)}) copy-start(bf16[2048,1024]{1,0:T(8,128)(2,1)} %eigvec.1) | copy-start | bytes 12582916

commit v5 on v4

--- a/solution.py
+++ b/solution.py
@@ -110,6 +110,11 @@
     return got[:, :rows], got[:, rows : rows + 1]
 
 
+def scaled_sum(terms, exponents):
+    top = exponents.max(0) + math.log2(terms.shape[0])
+    return (terms * jnp.exp2(exponents - top)).sum(0), top
+
+
 def shards(observed, prior_mean, missing, eigvec, lam_space, lam_time):
     stations, eigs = eigvec.shape
     pieces = lax.axis_size(PAIR)
@@ -124,9 +129,8 @@
     split = kernel_call(
         split_kernel, jax.ShapeDtypeStruct((pieces, COLS + EXTRA, share), jnp.float32), [VMEM], eigs * COLS, 8 * eigs * COLS
     )(proj)
-    terms, exponents = exchange(split, PAIR)
-    top = exponents.max(0) + math.log2(pieces)
-    half = jnp.concatenate([(terms * jnp.exp2(exponents - top)).sum(0), jnp.broadcast_to(top, (EXTRA, share))])
+    half, top = scaled_sum(*exchange(split, PAIR))
+    half = jnp.concatenate([half, jnp.broadcast_to(top, (EXTRA, share))])
     halves = lax.all_gather(half.astype(jnp.float16), "zh").astype(jnp.float32)
     coeffs = kernel_call(
         shrink_kernel, jax.ShapeDtypeStruct((share, COLS), jnp.bfloat16), [VMEM] * 4, 4 * COLS * COLS * share, COLS * COLS * 8
@@ -140,9 +144,10 @@
         nbytes,
         scratch,
     )(eigvec, gather(coeffs, PAIR))
-    terms, exponents = exchange(part, NEAR)
-    joined = (terms * jnp.exp2(exponents)).sum(0).astype(jnp.bfloat16).reshape(far, -1, COLS)
-    return lax.all_to_all(joined, "za", 0, 0).astype(jnp.float32).sum(0)
+    joined, top = scaled_sum(*exchange(part, NEAR))
+    joined = joined.reshape(far, -1, COLS)
+    terms, exponents = exchange(jnp.concatenate([joined, jnp.broadcast_to(top, (far, EXTRA, COLS))], axis=1), "za")
+    return (terms * jnp.exp2(exponents)).sum(0)
 
 
 def solution(mesh):

time: 104 us -> 105 us (level)
    all_to_all x2 -> x3, blocking collectives: 25.5 us -> 39.1 us  [exchange(): lax.all_to_all(pieces.astype(jnp.float16), axes, 0, 0).astype(jnp.float32)]
    all_to_all x1 -> x0, blocking collectives: 13.2 us -> none  [shards(): return lax.all_to_all(joined, 'za', 0, 0).astype(jnp.float32).sum(0)]
where the time goes in v5:
time: 105 us; the launch traced here: 104 us
  blocking collectives  96.6 us (92%)
  matrix products  2.95 us (3%)
  Pallas kernels  2.48 us (2%)
  other arithmetic  1.96 us (2%)
    all_to_all x3, blocking collectives, gather(): lax.all_to_all(copies, axes, 0, 0)  44.2 us
    all_to_all x3, blocking collectives, exchange(): lax.all_to_all(pieces.astype(jnp.float16), axes, 0, 0).astype(jnp.float32)  39.1 us
    all_gather x1, blocking collectives, shards(): halves = lax.all_gather(half.astype(jnp.float16), 'zh').astype(jnp.float32)  13.3 us
    dot_general x1, matrix products, shards(): lax.dot_general(filled, eigvec, (((0,), (0,)), ((), ())), preferred_eleme...  2.95 us

profile of v5, /device:TPU:2, one launch (start us, length us, event | category | flops | bytes accessed | tf_op | source)
XLA Modules:
  0.0 104.4 jit_solution(925103423033372057)
XLA Ops:
  0.0 0.8 compare_select_fusion
  0.8 21.1 %all_to_all.30 = bf16[4,64,128]{2,1,0:T(8,128)(2,1)S(1)} all-to-all(bf16[4,64,128]{2,1,0:T(8,128)(2,1)S(1)} %broadcast_in_dim.10), channel_id=1, replica_groups=mesh['y'=4,'zh'=2,'core'=2,'x'=4,'za'=4,'zc'=2] {'za'}, dimensions={0} | all-to-all | bytes 131072 | tf_op jit(solution)/shard_map/all_to_all | solution.py:104
  21.9 0.1 broadcast_in_dim.22
  22.0 12.7 %all_to_all.31 = bf16[8,256,128]{2,1,0:T(8,128)(2,1)S(1)} all-to-all(bf16[8,256,128]{2,1,0:T(8,128)(2,1)S(1)} %broadcast_in_dim.22), channel_id=1, replica_groups=mesh['y'=4,'zh'=2,'core'=2,'x'=4,'za'=4,'zc'=2] {'x','zc'}, dimensions={0} | all-to-all | bytes 1048576 | tf_op jit(solution)/shard_map/all_to_all | solution.py:104
  34.7 2.9 %fusion.6.proj = f32[128,1024]{1,0:T(8,128)S(1)} fusion(bf16[2048,128]{1,0:T(8,128)(2,1)S(1)} %bitcast.19, bf16[2048,1024]{1,0:T(8,128)(2,1)} %eigvec.1), kind=kOutput, calls=%fused_computation.20 | convolution fusion | flops 536870912 | bytes 5242880 | tf_op jit(solution)/shard_map/dot_general | solution.py:128
  37.6 0.0 copy-start.1
  37.6 0.0 copy-start.2
  37.7 0.0 copy-start.3
  37.7 0.2 shard_map.73
  37.9 0.0 copy-start
  37.9 12.2 %all_to_all.32 = f16[8,136,128]{2,1,0:T(8,128)(2,1)S(1)} all-to-all(f16[8,136,128]{2,1,0:T(8,128)(2,1)S(1)} %convert_element_type.27), channel_id=1, replica_groups=mesh['y'=4,'zh'=2,'core'=2,'x'=4,'za'=4,'zc'=2] {'y','core'}, dimensions={0} | all-to-all | bytes 557056 | tf_op jit(solution)/shard_map/all_to_all | solution.py:108
  50.4 13.3 %all_gather.4 = f16[2,136,128]{2,1,0:T(8,128)(2,1)S(1)} all-gather(f16[1,136,128]{2,1,0:T(8,128)(2,1)S(1)} %pad_maximum_fusion.1), channel_id=1, replica_groups=mesh['y'=4,'zh'=2,'core'=2,'x'=4,'za'=4,'zc'=2] {'zh'}, dimensions={0}, use_global_device_ids=true | all-gather | bytes 104448 | tf_op jit(solution)/shard_map/all_gather | solution.py:134
  63.7 0.0 copy-done.1
  63.7 0.0 copy-done.2
  63.7 0.0 copy-done.3
  63.7 0.5 shard_map.74
  64.3 10.5 %all_to_all.33 = bf16[8,128,128]{2,1,0:T(8,128)(2,1)S(1)} all-to-all(bf16[8,128,128]{2,1,0:T(8,128)(2,1)S(1)} %broadcast_in_dim.24), channel_id=1, replica_groups=mesh['y'=4,'zh'=2,'core'=2,'x'=4,'za'=4,'zc'=2] {'y','core'}, dimensions={0} | all-to-all | bytes 524288 | tf_op jit(solution)/shard_map/all_to_all | solution.py:104
  74.8 0.0 copy-done
  74.8 1.7 %shard_map.75 = f32[8,264,128]{2,1,0:T(8,128)S(1)} custom-call(bf16[2048,1024]{1,0:T(8,128)(2,1)S(1)} %copy-done, bf16[1024,128]{1,0:T(8,128)(2,1)S(1)} %bitcast.16), custom_call_target="tpu_custom_call" | custom-call | flops 536870912 | bytes 4194304 | tf_op jit(solution)/shard_map/pallas_call | solution.py:139
  76.6 0.1 convert_element_type.30
  76.6 13.5 %all_to_all.34 = f16[8,264,128]{2,1,0:T(8,128)(2,1)S(1)} all-to-all(f16[8,264,128]{2,1,0:T(8,128)(2,1)S(1)} %convert_element_type.30), channel_id=1, replica_groups=mesh['y'=4,'zh'=2,'core'=2,'x'=4,'za'=4,'zc'=2] {'x','zc'}, dimensions={0} | all-to-all | bytes 1081344 | tf_op jit(solution)/shard_map/all_to_all | solution.py:108
  90.2 0.1 convert_element_type.31
  90.3 0.1 fusion
  90.4 13.3 %all_to_all.35 = f16[4,72,128]{2,1,0:T(8,128)(2,1)S(1)} all-to-all(f16[4,72,128]{2,1,0:T(8,128)(2,1)S(1)} %pad_maximum_fusion), channel_id=1, replica_groups=mesh['y'=4,'zh'=2,'core'=2,'x'=4,'za'=4,'zc'=2] {'za'}, dimensions={0} | all-to-all | bytes 147456 | tf_op jit(solution)/shard_map/all_to_all | solution.py:108
  103.8 0.6 fusion.2
  (21 shorter events, 0.4 us)
Async XLA Ops:
  37.6 26.1 %copy-start.1 = (f32[128,128]{1,0:T(8,128)S(1)}, f32[128,128]{1,0:T(8,128)}, u32[]{:S(2)}) copy-start(f32[128,128]{1,0:T(8,128)} %constant.5.clone.table) | copy-start | bytes 196612
  37.6 26.1 %copy-start.2 = (f32[1024]{0:T(1024)S(1)}, f32[1024]{0:T(1024)}, u32[]{:S(2)}) copy-start(f32[1024]{0:T(1024)} %param.11) | copy-start | bytes 12292
  37.7 26.1 %copy-start.3 = (f32[32]{0:T(128)S(1)}, f32[32]{0:T(128)}, u32[]{:S(2)}) copy-start(f32[32]{0:T(128)} %param.12) | copy-start | bytes 388
  37.9 36.9 %copy-start = (bf16[2048,1024]{1,0:T(8,128)(2,1)S(1)}, bf16[2048,1024]{1,0:T(8,128)(2,1)}, u32[]{:S(2)}) copy-start(bf16[2048,1024]{1,0:T(8,128)(2,1)} %eigvec.1) | copy-start | bytes 12582916

commit v6 on v5

--- a/solution.py
+++ b/solution.py
@@ -50,10 +50,9 @@
     return held[...]
 
 
-def scaled(values):
+def exponent_of(values):
     largest = jnp.maximum(jnp.max(jnp.abs(values), keepdims=True), 1e-30)
-    exponent = jnp.floor(jnp.log(largest) * (1 / math.log(2.0))) - TOP
-    return values * jnp.exp2(-exponent), exponent
+    return jnp.floor(jnp.log(largest) * (1 / math.log(2.0))) - TOP
 
 
 def put_exponent(out, exponent):
@@ -62,11 +61,10 @@
 
 
 def split_kernel(proj, out):
-    proj, exponent = scaled(proj[...])
     size = out.shape[2]
     for piece in range(out.shape[0]):
         out[piece, :COLS, :] = proj[:, piece * size : (piece + 1) * size]
-    put_exponent(out, exponent)
+    put_exponent(out, exponent_of(proj[...]))
 
 
 def shrink_kernel(halves, table, lam_space, lam_time, out):
@@ -89,13 +87,13 @@
 
 
 def smooth_kernel(far, eigvec, coeffs, out, held, sem):
-    part, exponent = scaled(jnp.dot(fetched(eigvec, held, sem), coeffs[...], preferred_element_type=jnp.float32))
+    part = jnp.dot(fetched(eigvec, held, sem), coeffs[...], preferred_element_type=jnp.float32)
     size = part.shape[0] // (out.shape[0] * far)
     for block in range(part.shape[0] // size):
         piece = block // (2 * far) * 2 + block % 2
         start = block // 2 % far * size
         out[piece, start : start + size, :] = part[block * size : (block + 1) * size]
-    put_exponent(out, exponent)
+    put_exponent(out, exponent_of(part))
 
 
 def gather(block, axes):
@@ -108,6 +106,12 @@
     got = lax.all_to_all(pieces.astype(jnp.float16), axes, 0, 0).astype(jnp.float32)
     rows = got.shape[1] - EXTRA
     return got[:, :rows], got[:, rows : rows + 1]
+
+
+def scaled(pieces):
+    rows = pieces.shape[1] - EXTRA
+    row = lax.broadcasted_iota(jnp.int32, pieces.shape, 1)
+    return jnp.where(row < rows, pieces * jnp.exp2(-pieces[:, rows : rows + 1]), pieces)
 
 
 def scaled_sum(terms, exponents):
@@ -129,7 +133,7 @@
     split = kernel_call(
         split_kernel, jax.ShapeDtypeStruct((pieces, COLS + EXTRA, share), jnp.float32), [VMEM], eigs * COLS, 8 * eigs * COLS
     )(proj)
-    half, top = scaled_sum(*exchange(split, PAIR))
+    half, top = scaled_sum(*exchange(scaled(split), PAIR))
     half = jnp.concatenate([half, jnp.broadcast_to(top, (EXTRA, share))])
     halves = lax.all_gather(half.astype(jnp.float16), "zh").astype(jnp.float32)
     coeffs = kernel_call(
@@ -144,7 +148,7 @@
         nbytes,
         scratch,
     )(eigvec, gather(coeffs, PAIR))
-    joined, top = scaled_sum(*exchange(part, NEAR))
+    joined, top = scaled_sum(*exchange(scaled(part), NEAR))
     joined = joined.reshape(far, -1, COLS)
     terms, exponents = exchange(jnp.concatenate([joined, jnp.broadcast_to(top, (far, EXTRA, COLS))], axis=1), "za")
     return (terms * jnp.exp2(exponents)).sum(0)

time: 105 us -> 109 us (1.038)
  blocking collectives: 96.6 us -> 86.4 us
  waiting for transfers between devices: 0 us -> 7.45 us
  starting transfers between devices: 0 us -> 3.41 us
  local copies, waits for them, and re-layouts: 0.19 us -> 3.05 us
    all_to_all x3 -> x2, blocking collectives: 44.2 us -> 33.7 us  [gather(): lax.all_to_all(copies, axes, 0, 0)]
    all_to_all x0 -> x1, waiting for transfers between devices: none -> 7.45 us  [gather(): lax.all_to_all(copies, axes, 0, 0)]
    all_to_all x0 -> x1, starting transfers between devices: none -> 3.41 us  [gather(): lax.all_to_all(copies, axes, 0, 0)]
    unnamed x8, local copies, waits for them, and re-layouts: 0.03 us -> 2.2 us
  transfers between devices with their start and end apart: 0 -> 1, of which waited for: 0 -> 1; matrix products, arithmetic and copies ran while one was open for 0% -> 0% of each run, Pallas kernels for 0% -> 0%
where the time goes in v6:
time: 109 us; the launch traced here: 108 us
  blocking collectives  86.4 us (79%)
  waiting for transfers between devices  7.45 us (7%)
  starting transfers between devices  3.41 us (3%)
  local copies, waits for them, and re-layouts  3.05 us (3%)
  matrix products  2.95 us (3%)
  Pallas kernels  2.36 us (2%)
  other arithmetic  2.21 us (2%)
    all_to_all x3, blocking collectives, exchange(): lax.all_to_all(pieces.astype(jnp.float16), axes, 0, 0).astype(jnp.float32)  39.4 us
    all_to_all x2, blocking collectives, gather(): lax.all_to_all(copies, axes, 0, 0)  33.7 us
    all_gather x1, blocking collectives, shards(): halves = lax.all_gather(half.astype(jnp.float16), 'zh').astype(jnp.float32)  13.3 us
    all_to_all x1, waiting for transfers between devices, gather(): lax.all_to_all(copies, axes, 0, 0)  7.45 us
    all_to_all x1, starting transfers between devices, gather(): lax.all_to_all(copies, axes, 0, 0)  3.41 us
    dot_general x1, matrix products, shards(): lax.dot_general(filled, eigvec, (((0,), (0,)), ((), ())), preferred_eleme...  2.95 us
    unnamed x8, local copies, waits for them, and re-layouts  2.2 us
  transfers between devices with their start and end apart: 1, of which 1 were waited for; matrix products, arithmetic and copies ran while one was open for 0% of the time, Pallas kernels for 0%

profile of v6, /device:TPU:2, one launch (start us, length us, event | category | flops | bytes accessed | tf_op | source)
XLA Modules:
  0.0 108.1 jit_solution(13305014571820836925)
XLA Ops:
  0.0 0.8 compare_select_fusion
  0.8 21.1 %all_to_all.30 = bf16[4,64,128]{2,1,0:T(8,128)(2,1)S(1)} all-to-all(bf16[4,64,128]{2,1,0:T(8,128)(2,1)S(1)} %broadcast_in_dim.10), channel_id=1, replica_groups=mesh['y'=4,'zh'=2,'core'=2,'x'=4,'za'=4,'zc'=2] {'za'}, dimensions={0} | all-to-all | bytes 131072 | tf_op jit(solution)/shard_map/all_to_all | solution.py:102
  21.9 0.1 broadcast_in_dim.22
  22.0 12.7 %all_to_all.31 = bf16[8,256,128]{2,1,0:T(8,128)(2,1)S(1)} all-to-all(bf16[8,256,128]{2,1,0:T(8,128)(2,1)S(1)} %broadcast_in_dim.22), channel_id=1, replica_groups=mesh['y'=4,'zh'=2,'core'=2,'x'=4,'za'=4,'zc'=2] {'x','zc'}, dimensions={0} | all-to-all | bytes 1048576 | tf_op jit(solution)/shard_map/all_to_all | solution.py:102
  34.7 2.9 %fusion.12.proj = f32[128,1024]{1,0:T(8,128)S(1)} fusion(bf16[2048,128]{1,0:T(8,128)(2,1)S(1)} %bitcast.21, bf16[2048,1024]{1,0:T(8,128)(2,1)} %eigvec.1), kind=kOutput, calls=%fused_computation.32 | convolution fusion | flops 536870912 | bytes 5242880 | tf_op jit(solution)/shard_map/dot_general | solution.py:132
  37.6 0.2 shard_map.73
  37.8 0.1 fusion.2
  38.0 12.0 %all_to_all.32 = f16[8,136,128]{2,1,0:T(8,128)(2,1)S(1)} all-to-all(f16[8,136,128]{2,1,0:T(8,128)(2,1)S(1)} %fusion.2), channel_id=1, replica_groups=mesh['y'=4,'zh'=2,'core'=2,'x'=4,'za'=4,'zc'=2] {'y','core'}, dimensions={0} | all-to-all | bytes 557056 | tf_op jit(solution)/shard_map/all_to_all | solution.py:106
  49.9 0.0 copy-start.1
  49.9 0.0 copy-start.2
  49.9 0.0 copy-start.3
  50.1 13.3 %all_gather.4 = f16[2,136,128]{2,1,0:T(8,128)(2,1)S(1)} all-gather(f16[1,136,128]{2,1,0:T(8,128)(2,1)S(1)} %pad_maximum_fusion.1), channel_id=1, replica_groups=mesh['y'=4,'zh'=2,'core'=2,'x'=4,'za'=4,'zc'=2] {'zh'}, dimensions={0}, use_global_device_ids=true | all-gather | bytes 104448 | tf_op jit(solution)/shard_map/all_gather | solution.py:138
  63.5 0.0 copy-done.1
  63.5 0.0 copy-done.2
  63.5 0.0 copy-done.3
  63.5 0.5 shard_map.74
  64.1 0.7 broadcast_in_dim.24
  64.8 3.4 %all-to-all-start.3 = ((bf16[8,128,128]{2,1,0:T(8,128)(2,1)}), bf16[8,128,128]{2,1,0:T(8,128)(2,1)S(1)}, u32[]{:S(2)}, u32[]{:S(2)}) async-start(bf16[8,128,128]{2,1,0:T(8,128)(2,1)} %broadcast_in_dim.24), calls=%async_computation.3 | async-start | bytes 524288 | tf_op jit(solution)/shard_map/all_to_all | solution.py:102
  68.2 7.4 %all-to-all-done.3 = bf16[8,128,128]{2,1,0:T(8,128)(2,1)S(1)} async-done(((bf16[8,128,128]{2,1,0:T(8,128)(2,1)}), bf16[8,128,128]{2,1,0:T(8,128)(2,1)S(1)}, u32[]{:S(2)}, u32[]{:S(2)}) %all-to-all-start.3) | async-done | bytes 262176 | tf_op jit(solution)/shard_map/all_to_all | solution.py:102
  75.7 0.0 copy-start
  75.7 2.2 %copy-done = bf16[2048,1024]{1,0:T(8,128)(2,1)S(1)} copy-done((bf16[2048,1024]{1,0:T(8,128)(2,1)S(1)}, bf16[2048,1024]{1,0:T(8,128)(2,1)}, u32[]{:S(2)}) %copy-start) | copy-done | bytes 4194328
  77.9 1.7 %shard_map.75 = f32[8,264,128]{2,1,0:T(8,128)S(1)} custom-call(bf16[2048,1024]{1,0:T(8,128)(2,1)S(1)} %copy-done, bf16[1024,128]{1,0:T(8,128)(2,1)S(1)} %bitcast.18), custom_call_target="tpu_custom_call" | custom-call | flops 536870912 | bytes 4194304 | tf_op jit(solution)/shard_map/pallas_call | solution.py:143
  79.6 0.2 fusion
  79.8 14.0 %all_to_all.33 = f16[8,264,128]{2,1,0:T(8,128)(2,1)S(1)} all-to-all(f16[8,264,128]{2,1,0:T(8,128)(2,1)S(1)} %fusion), channel_id=1, replica_groups=mesh['y'=4,'zh'=2,'core'=2,'x'=4,'za'=4,'zc'=2] {'x','zc'}, dimensions={0} | all-to-all | bytes 1081344 | tf_op jit(solution)/shard_map/all_to_all | solution.py:106
  93.8 0.1 convert_element_type.31
  93.9 0.1 fusion.1
  94.1 13.3 %all_to_all.34 = f16[4,72,128]{2,1,0:T(8,128)(2,1)S(1)} all-to-all(f16[4,72,128]{2,1,0:T(8,128)(2,1)S(1)} %pad_maximum_fusion), channel_id=1, replica_groups=mesh['y'=4,'zh'=2,'core'=2,'x'=4,'za'=4,'zc'=2] {'za'}, dimensions={0} | all-to-all | bytes 147456 | tf_op jit(solution)/shard_map/all_to_all | solution.py:106
  107.5 0.6 fusion.4
  (23 shorter events, 0.4 us)
Async XLA Ops:
  49.9 13.6 %copy-start.1 = (f32[128,128]{1,0:T(8,128)S(1)}, f32[128,128]{1,0:T(8,128)}, u32[]{:S(2)}) copy-start(f32[128,128]{1,0:T(8,128)} %constant.7.clone.table) | copy-start | bytes 196612
  49.9 13.6 %copy-start.2 = (f32[1024]{0:T(1024)S(1)}, f32[1024]{0:T(1024)}, u32[]{:S(2)}) copy-start(f32[1024]{0:T(1024)} %param.11) | copy-start | bytes 12292
  49.9 13.6 %copy-start.3 = (f32[32]{0:T(128)S(1)}, f32[32]{0:T(128)}, u32[]{:S(2)}) copy-start(f32[32]{0:T(128)} %param.12) | copy-start | bytes 388
  64.8 10.9 %all-to-all-start.3 = ((bf16[8,128,128]{2,1,0:T(8,128)(2,1)}), bf16[8,128,128]{2,1,0:T(8,128)(2,1)S(1)}, u32[]{:S(2)}, u32[]{:S(2)}) async-start(bf16[8,128,128]{2,1,0:T(8,128)(2,1)} %broadcast_in_dim.24), calls=%async_computation.3 | async-start | bytes 524288 | tf_op jit(solution)/shard_map/all_to_all | solution.py:102
  75.7 2.2 %copy-start = (bf16[2048,1024]{1,0:T(8,128)(2,1)S(1)}, bf16[2048,1024]{1,0:T(8,128)(2,1)}, u32[]{:S(2)}) copy-start(bf16[2048,1024]{1,0:T(8,128)(2,1)} %eigvec.1) | copy-start | bytes 12582916

commit v7 on v5

--- a/solution.py
+++ b/solution.py
@@ -38,7 +38,7 @@
         in_specs=in_specs,
         out_specs=VMEM,
         scratch_shapes=scratch_shapes,
-        compiler_params=pltpu.CompilerParams(vmem_limit_bytes=12 * 2**20),
+        compiler_params=pltpu.CompilerParams(vmem_limit_bytes=8 * 2**20),
         cost_estimate=pl.CostEstimate(flops=flops, bytes_accessed=nbytes, transcendentals=0),
     )
 

time: 105 us -> 105 us (level)
  no operation moved by 1% of the time
where the time goes in v7:
time: 105 us; the launch traced here: 104 us
  blocking collectives  96.6 us (92%)
  matrix products  2.95 us (3%)
  Pallas kernels  2.48 us (2%)
  other arithmetic  1.96 us (2%)
    all_to_all x3, blocking collectives, gather(): lax.all_to_all(copies, axes, 0, 0)  44.2 us
    all_to_all x3, blocking collectives, exchange(): lax.all_to_all(pieces.astype(jnp.float16), axes, 0, 0).astype(jnp.float32)  39.1 us
    all_gather x1, blocking collectives, shards(): halves = lax.all_gather(half.astype(jnp.float16), 'zh').astype(jnp.float32)  13.3 us
    dot_general x1, matrix products, shards(): lax.dot_general(filled, eigvec, (((0,), (0,)), ((), ())), preferred_eleme...  2.95 us

profile of v7, /device:TPU:2, one launch (start us, length us, event | category | flops | bytes accessed | tf_op | source)
XLA Modules:
  0.0 104.4 jit_solution(2186504391748633955)
XLA Ops:
  0.0 0.8 compare_select_fusion
  0.8 21.1 %all_to_all.30 = bf16[4,64,128]{2,1,0:T(8,128)(2,1)S(1)} all-to-all(bf16[4,64,128]{2,1,0:T(8,128)(2,1)S(1)} %broadcast_in_dim.10), channel_id=1, replica_groups=mesh['y'=4,'zh'=2,'core'=2,'x'=4,'za'=4,'zc'=2] {'za'}, dimensions={0} | all-to-all | bytes 131072 | tf_op jit(solution)/shard_map/all_to_all | solution.py:104
  21.9 0.1 broadcast_in_dim.22
  22.0 12.7 %all_to_all.31 = bf16[8,256,128]{2,1,0:T(8,128)(2,1)S(1)} all-to-all(bf16[8,256,128]{2,1,0:T(8,128)(2,1)S(1)} %broadcast_in_dim.22), channel_id=1, replica_groups=mesh['y'=4,'zh'=2,'core'=2,'x'=4,'za'=4,'zc'=2] {'x','zc'}, dimensions={0} | all-to-all | bytes 1048576 | tf_op jit(solution)/shard_map/all_to_all | solution.py:104
  34.7 2.9 %fusion.6.proj = f32[128,1024]{1,0:T(8,128)S(1)} fusion(bf16[2048,128]{1,0:T(8,128)(2,1)S(1)} %bitcast.19, bf16[2048,1024]{1,0:T(8,128)(2,1)} %eigvec.1), kind=kOutput, calls=%fused_computation.20 | convolution fusion | flops 536870912 | bytes 5242880 | tf_op jit(solution)/shard_map/dot_general | solution.py:128
  37.6 0.0 copy-start.1
  37.6 0.0 copy-start.2
  37.7 0.0 copy-start.3
  37.7 0.2 shard_map.73
  37.9 0.0 copy-start
  37.9 12.2 %all_to_all.32 = f16[8,136,128]{2,1,0:T(8,128)(2,1)S(1)} all-to-all(f16[8,136,128]{2,1,0:T(8,128)(2,1)S(1)} %convert_element_type.27), channel_id=1, replica_groups=mesh['y'=4,'zh'=2,'core'=2,'x'=4,'za'=4,'zc'=2] {'y','core'}, dimensions={0} | all-to-all | bytes 557056 | tf_op jit(solution)/shard_map/all_to_all | solution.py:108
  50.4 13.3 %all_gather.4 = f16[2,136,128]{2,1,0:T(8,128)(2,1)S(1)} all-gather(f16[1,136,128]{2,1,0:T(8,128)(2,1)S(1)} %pad_maximum_fusion.1), channel_id=1, replica_groups=mesh['y'=4,'zh'=2,'core'=2,'x'=4,'za'=4,'zc'=2] {'zh'}, dimensions={0}, use_global_device_ids=true | all-gather | bytes 104448 | tf_op jit(solution)/shard_map/all_gather | solution.py:134
  63.7 0.0 copy-done.1
  63.7 0.0 copy-done.2
  63.7 0.0 copy-done.3
  63.7 0.5 shard_map.74
  64.3 10.5 %all_to_all.33 = bf16[8,128,128]{2,1,0:T(8,128)(2,1)S(1)} all-to-all(bf16[8,128,128]{2,1,0:T(8,128)(2,1)S(1)} %broadcast_in_dim.24), channel_id=1, replica_groups=mesh['y'=4,'zh'=2,'core'=2,'x'=4,'za'=4,'zc'=2] {'y','core'}, dimensions={0} | all-to-all | bytes 524288 | tf_op jit(solution)/shard_map/all_to_all | solution.py:104
  74.8 0.0 copy-done
  74.8 1.7 %shard_map.75 = f32[8,264,128]{2,1,0:T(8,128)S(1)} custom-call(bf16[2048,1024]{1,0:T(8,128)(2,1)S(1)} %copy-done, bf16[1024,128]{1,0:T(8,128)(2,1)S(1)} %bitcast.16), custom_call_target="tpu_custom_call" | custom-call | flops 536870912 | bytes 4194304 | tf_op jit(solution)/shard_map/pallas_call | solution.py:139
  76.6 0.1 convert_element_type.30
  76.6 13.5 %all_to_all.34 = f16[8,264,128]{2,1,0:T(8,128)(2,1)S(1)} all-to-all(f16[8,264,128]{2,1,0:T(8,128)(2,1)S(1)} %convert_element_type.30), channel_id=1, replica_groups=mesh['y'=4,'zh'=2,'core'=2,'x'=4,'za'=4,'zc'=2] {'x','zc'}, dimensions={0} | all-to-all | bytes 1081344 | tf_op jit(solution)/shard_map/all_to_all | solution.py:108
  90.2 0.1 convert_element_type.31
  90.3 0.1 fusion
  90.4 13.3 %all_to_all.35 = f16[4,72,128]{2,1,0:T(8,128)(2,1)S(1)} all-to-all(f16[4,72,128]{2,1,0:T(8,128)(2,1)S(1)} %pad_maximum_fusion), channel_id=1, replica_groups=mesh['y'=4,'zh'=2,'core'=2,'x'=4,'za'=4,'zc'=2] {'za'}, dimensions={0} | all-to-all | bytes 147456 | tf_op jit(solution)/shard_map/all_to_all | solution.py:108
  103.8 0.6 fusion.2
  (21 shorter events, 0.4 us)
Async XLA Ops:
  37.6 26.1 %copy-start.1 = (f32[128,128]{1,0:T(8,128)S(1)}, f32[128,128]{1,0:T(8,128)}, u32[]{:S(2)}) copy-start(f32[128,128]{1,0:T(8,128)} %constant.5.clone.table) | copy-start | bytes 196612
  37.6 26.1 %copy-start.2 = (f32[1024]{0:T(1024)S(1)}, f32[1024]{0:T(1024)}, u32[]{:S(2)}) copy-start(f32[1024]{0:T(1024)} %param.11) | copy-start | bytes 12292
  37.7 26.1 %copy-start.3 = (f32[32]{0:T(128)S(1)}, f32[32]{0:T(128)}, u32[]{:S(2)}) copy-start(f32[32]{0:T(128)} %param.12) | copy-start | bytes 388
  37.9 36.9 %copy-start = (bf16[2048,1024]{1,0:T(8,128)(2,1)S(1)}, bf16[2048,1024]{1,0:T(8,128)(2,1)}, u32[]{:S(2)}) copy-start(bf16[2048,1024]{1,0:T(8,128)(2,1)} %eigvec.1) | copy-start | bytes 12582916
